TPU v7x, 32 devices: a whole 2x2x4 slice. The times are simulated.
32 devices in a mesh: parts: 2 (over x), seq: 8 (over z, y), dp: 2 (over core).
Axes of the slice: x: 2, y: 2, z: 4, core: 2. Of those that a mesh axis runs over, the one named last changes fastest.
Arguments:
- queries: bfloat16 [4, 2048, 1024], P(('parts', 'dp'), 'seq'), parts along dimension 0, may hold values from -8 to 8
- key_states: bfloat16 [4, 2048, 1024], P(('parts', 'dp'), 'seq'), parts along dimension 0, may hold values from -8 to 8
- value_states: bfloat16 [4, 2048, 1024], P(('parts', 'dp'), 'seq'), parts along dimension 0, may hold values from -6 to 6
- out_grad: bfloat16 [4, 2048, 1024], P(('parts', 'dp'), 'seq'), parts along dimension 0, may hold values from -1.5 to 1.5
- layer_input: bfloat16 [4, 2048, 2048], P(('parts', 'dp'), 'seq'), parts along dimension 0, may hold values from -6 to 6
Outputs:
- weight_grad: float32 [4096, 1024], P(('parts', 'seq', 'dp')), parts along dimension 0
There are 2 independent parts, one for each index of `parts`. A program takes and returns all parts, laid end to end along the dimension named above; each array names one. Nothing has to cross between parts.
All inputs are finite; a program needn't handle non-finite values.
Results may differ from a plain program's by a relative error of at most 0.0041.
Values may be sent and summed in bfloat16 or wider, within the bound.
No kernel may reach another device: no remote copies, remote signals or barrier semaphores. Data moves between devices by JAX's collectives and lax.ppermute only.
A program may use at most 192 MiB of HBM per device.

v0:
```python
import math

import jax
import jax.numpy as jnp
from jax import lax
from jax.sharding import PartitionSpec as P

HEADS = 8
HEAD_DIM = 128
HALF = 1024


def shifted(value, axis, steps):
    count = lax.axis_size(axis)
    first, last = (max(0, -steps), min(count, count - steps))
    return lax.ppermute(value, axis, [(source, source + steps) for source in range(first, last)])


def dot_rows(left, right):
    return lax.dot_general(
        left, right, (((0,), (0,)), ((), ())), preferred_element_type=jnp.float32
    )


def window_grads(queries, key_value, out_grad, first_row, doc_length):
    rows_dev = queries.shape[0]
    inner_width = queries.shape[1]
    block_rows = min(rows_dev, 512)
    window = block_rows + 2 * HALF
    head_group = min(HEADS, 4)
    group_width = head_group * HEAD_DIM
    inverse_root = 1.0 / math.sqrt(HEAD_DIM)
    accumulated = jnp.zeros((rows_dev + 2 * HALF, inner_width), jnp.float32)
    offsets = jnp.arange(window)[None, :] - jnp.arange(block_rows)[:, None]
    position = first_row + 0 - HALF + jnp.arange(window)
    visible = (
        (offsets >= 0)
        & (offsets <= 2 * HALF)
        & (position >= 0)[None, :]
        & (position < doc_length)[None, :]
    )
    for first_head in range(0, HEADS, head_group):
        low_col = first_head * HEAD_DIM
        query_rows = queries[0:block_rows, low_col : low_col + group_width].reshape(
            block_rows, head_group, HEAD_DIM
        )
        grad_rows = out_grad[0:block_rows, low_col : low_col + group_width].reshape(
            block_rows, head_group, HEAD_DIM
        )
        key_rows = key_value[0:window, low_col : low_col + group_width].reshape(
            window, head_group, HEAD_DIM
        )
        value_rows = key_value[
            0:window, inner_width + low_col : inner_width + low_col + group_width
        ].reshape(window, head_group, HEAD_DIM)
        scores = (
            jnp.einsum("ihe,jhe->hij", query_rows, key_rows, preferred_element_type=jnp.float32)
            * inverse_root
        )
        scores = jnp.where(visible[None], scores, -1e30)
        row_max = jnp.max(scores, axis=2, keepdims=True)
        weights = jnp.where(visible[None], jnp.exp(scores - row_max), 0.0)
        probs = weights / jnp.sum(weights, axis=2, keepdims=True)
        dprobs = jnp.einsum(
            "ihe,jhe->hij", grad_rows, value_rows, preferred_element_type=jnp.float32
        )
        row_delta = jnp.sum(probs * dprobs, axis=2, keepdims=True)
        dscores = probs * (dprobs - row_delta)
        key_grad = (
            jnp.einsum(
                "hij,ihe->jhe",
                dscores.astype(jnp.bfloat16),
                query_rows,
                preferred_element_type=jnp.float32,
            )
            * inverse_root
        )
        accumulated = accumulated.at[0:window, low_col : low_col + group_width].add(
            key_grad.reshape(window, group_width)
        )
    return accumulated.astype(jnp.bfloat16)


def local(queries, key_states, value_states, out_grad, layer_input):
    rows_dev = queries.shape[1]
    model_width = layer_input.shape[2]
    seq_count = lax.axis_size("seq")
    pair_count = lax.axis_size("dp")
    share = model_width // (seq_count * pair_count)
    first_row = lax.axis_index("seq") * rows_dev
    doc_length = seq_count * rows_dev
    reach = HALF // rows_dev
    joined = jnp.concatenate([key_states, value_states], axis=2)
    earlier_rows = []
    for distance in range(reach, 0, -1):
        earlier_rows.append(shifted(joined, "seq", distance))
    later_rows = []
    for distance in range(1, reach + 1):
        later_rows.append(shifted(joined, "seq", -distance))
    extended = jnp.concatenate(earlier_rows + [joined] + later_rows, axis=1)
    partial_value = window_grads(queries[0], extended[0], out_grad[0], first_row, doc_length)
    received = []
    for distance in range(1, reach + 1):
        left_piece = partial_value[HALF - distance * rows_dev : HALF - (distance - 1) * rows_dev]
        received.append(shifted(left_piece, "seq", -distance))
        right_start = HALF + rows_dev + (distance - 1) * rows_dev
        right_piece = partial_value[right_start : right_start + rows_dev]
        received.append(shifted(right_piece, "seq", distance))
    local_part = partial_value[HALF : HALF + rows_dev]
    source = layer_input[0]
    shaped = source.reshape(source.shape[0], seq_count, pair_count, share)
    own_input = shaped.transpose(0, 2, 1, 3).reshape(source.shape[0], model_width)
    result = dot_rows(own_input, local_part)
    for piece in received:
        result = result + dot_rows(own_input, piece)
    halves = lax.psum_scatter(result, "dp", scatter_dimension=0, tiled=True)
    return lax.psum_scatter(halves, "seq", scatter_dimension=0, tiled=True)


def solution(mesh):
    in_specs = (
        P(("parts", "dp"), "seq", None),
        P(("parts", "dp"), "seq", None),
        P(("parts", "dp"), "seq", None),
        P(("parts", "dp"), "seq", None),
        P(("parts", "dp"), "seq", None),
    )
    out_specs = P(("parts", "seq", "dp"), None)
    return jax.shard_map(local, mesh=mesh, in_specs=in_specs, out_specs=out_specs, check_vma=False)
```

profile of v0, /device:TPU:0, one launch (start us, length us, event | category | flops | bytes accessed | tf_op | source)
XLA Modules:
  0.0 532.8 jit_solution(14964219859740009739)
XLA Ops:
  11.4 5.9 %collective-permute-start.3 = (bf16[1,256,2048]{1,2,0:T(8,128)(2,1)}, bf16[1,256,2048]{1,2,0:T(8,128)(2,1)}, u32[]{:S(2)}, u32[]{:S(2)}) collective-permute-start(bf16[1,256,2048]{1,2,0:T(8,128)(2,1)} %pad_maximum_fusion), channel_id=1, source_target_pairs={{0,2},{2,4},{4,6},{6,8},{8,10},{10,12},{12,14},{1,3},{3,5},{5,7},{... | collective-permute-start | bytes 3145736 | tf_op jit(solution)/shard_map/ppermute | solution.py:16
  17.2 3.5 collective-permute-start.2
  20.7 5.5 %collective-permute-start.1 = (bf16[1,256,2048]{1,2,0:T(8,128)(2,1)}, bf16[1,256,2048]{1,2,0:T(8,128)(2,1)}, u32[]{:S(2)}, u32[]{:S(2)}) collective-permute-start(bf16[1,256,2048]{1,2,0:T(8,128)(2,1)} %pad_maximum_fusion), channel_id=1, source_target_pairs={{0,6},{2,8},{4,10},{6,12},{8,14},{1,7},{3,9},{5,11},{7,13},{9,15},... | collective-permute-start | bytes 3145736 | tf_op jit(solution)/shard_map/ppermute | solution.py:16
  26.2 2.2 collective-permute-start
  35.0 52.2 %collective-permute-done = bf16[1,256,2048]{1,2,0:T(8,128)(2,1)} collective-permute-done((bf16[1,256,2048]{1,2,0:T(8,128)(2,1)}, bf16[1,256,2048]{1,2,0:T(8,128)(2,1)}, u32[]{:S(2)}, u32[]{:S(2)}) %collective-permute-start) | collective-permute-done | bytes 1048608 | tf_op jit(solution)/shard_map/ppermute | solution.py:16
  96.5 35.8 %collective-permute-done.4 = bf16[1,256,2048]{1,2,0:T(8,128)(2,1)S(1)} collective-permute-done((bf16[1,256,2048]{1,2,0:T(8,128)(2,1)}, bf16[1,256,2048]{1,2,0:T(8,128)(2,1)S(1)}, u32[]{:S(2)}, u32[]{:S(2)}) %collective-permute-start.4) | collective-permute-done | bytes 1048608 | tf_op jit(solution)/shard_map/ppermute | solution.py:16
  132.4 25.7 %collective-permute-done.5 = bf16[1,256,2048]{1,2,0:T(8,128)(2,1)S(1)} collective-permute-done((bf16[1,256,2048]{1,2,0:T(8,128)(2,1)}, bf16[1,256,2048]{1,2,0:T(8,128)(2,1)S(1)}, u32[]{:S(2)}, u32[]{:S(2)}) %collective-permute-start.5) | collective-permute-done | bytes 1048608 | tf_op jit(solution)/shard_map/ppermute | solution.py:16
  158.2 45.8 %collective-permute-done.6 = bf16[1,256,2048]{1,2,0:T(8,128)(2,1)S(1)} collective-permute-done((bf16[1,256,2048]{1,2,0:T(8,128)(2,1)}, bf16[1,256,2048]{1,2,0:T(8,128)(2,1)S(1)}, u32[]{:S(2)}, u32[]{:S(2)}) %collective-permute-start.6) | collective-permute-done | bytes 1048608 | tf_op jit(solution)/shard_map/ppermute | solution.py:16
  204.2 3.0 fusion.53
  207.2 9.7 %fusion.56 = (f32[4,256]{1,0:T(4,128)S(1)}, f32[4,256,2304]{1,2,0:T(8,128)}) fusion(pred[256,2304]{0,1:T(8,128)(4,1)S(1)} %fusion.31, bf16[2304,4,128]{0,2,1:T(8,128)(2,1)} %bitcast.106, bf16[256,4,128]{0,2,1:T(8,128)(2,1)S(1)} %bitcast.109), kind=kOutput, calls=%fused_computation.90 | convolution fusion | flops 615778560 | bytes 12652544 | tf_op jit(solution)/shard_map/sub | solution.py:62
  216.8 9.6 %fusion.57 = (f32[4,256]{1,0:T(4,128)S(1)}, f32[4,256,2304]{1,2,0:T(8,128)}) fusion(pred[256,2304]{0,1:T(8,128)(4,1)S(1)} %fusion.31, bf16[2304,4,128]{0,2,1:T(8,128)(2,1)} %bitcast.105, bf16[256,4,128]{0,2,1:T(8,128)(2,1)S(1)} %bitcast.113), kind=kOutput, calls=%fused_computation.91 | convolution fusion | flops 615778560 | bytes 12652544 | tf_op jit(solution)/shard_map/sub | solution.py:62
  226.5 6.9 %fusion.2 = (f32[4,256]{1,0:T(4,128)S(1)}, f32[4,2304,256]{2,1,0:T(8,128)}) fusion(f32[4,256,2304]{1,2,0:T(8,128)} %get-tuple-element.50, f32[4,256]{1,0:T(4,128)S(1)} %get-tuple-element.49, bf16[2304,4,128]{0,2,1:T(8,128)(2,1)S(1)} %bitcast.104, bf16[256,4,128]{0,2,1:T(8,128)(2,1)S(1)} %bitcast.114), kind=kOutput, calls=%fused_computation.4 | convolution fusion | flops 611056640 | bytes 21504000 | tf_op jit(solution)/shard_map/ihe,jhe->hij/dot_general | solution.py:64
  233.4 8.2 %fusion.21 = bf16[4,2304,128]{1,2,0:T(8,128)(2,1)S(1)} fusion(bf16[256,4,128]{0,2,1:T(8,128)(2,1)} %bitcast.112, f32[4,2304,256]{2,1,0:T(8,128)} %get-tuple-element.52, f32[4,256]{1,0:T(4,128)S(1)} %get-tuple-element.51, f32[4,256,2304]{1,2,0:T(8,128)} %get-tuple-element.50, f32[4,256]{1,0:T(4,128)S(1)} %get-tuple-element.49), kind=kOutput, calls=%fused_computation.48 | convolution fusion | flops 615776256 | bytes 21504000 | tf_op jit(solution)/shard_map/hij,ihe->jhe/dot_general | solution.py:70
  241.6 9.7 %fusion.5 = (f32[4,256]{1,0:T(4,128)S(1)}, f32[4,2304,256]{2,1,0:T(8,128)}) fusion(f32[4,256,2304]{1,2,0:T(8,128)} %get-tuple-element.46, f32[4,256]{1,0:T(4,128)S(1)} %get-tuple-element.45, bf16[2304,4,128]{0,2,1:T(8,128)(2,1)} %bitcast.103, bf16[256,4,128]{0,2,1:T(8,128)(2,1)S(1)} %bitcast.111), kind=kOutput, calls=%fused_computation.10 | convolution fusion | flops 611056640 | bytes 21504000 | tf_op jit(solution)/shard_map/ihe,jhe->hij/dot_general | solution.py:64
  251.2 10.2 %fusion.24 = bf16[4,2304,128]{1,2,0:T(8,128)(2,1)} fusion(bf16[256,4,128]{0,2,1:T(8,128)(2,1)S(1)} %bitcast.110, f32[4,2304,256]{2,1,0:T(8,128)} %get-tuple-element.48, f32[4,256]{1,0:T(4,128)S(1)} %get-tuple-element.47, f32[4,256,2304]{1,2,0:T(8,128)} %get-tuple-element.46, f32[4,256]{1,0:T(4,128)S(1)} %get-tuple-element.45, pred[]{:T(512)} %compare_reduce_fusion), kind=kOutput, calls=%fused_computation.49 | convolution fusion | flops 616955904 | bytes 21504000 | tf_op jit(solution)/shard_map/hij,ihe->jhe/dot_general | solution.py:70
  261.5 3.5 fusion.38
  270.2 46.9 %collective-permute-start.9 = (bf16[256,1024]{0,1:T(8,128)(2,1)}, bf16[256,1024]{0,1:T(8,128)(2,1)S(1)}, u32[]{:S(2)}, u32[]{:S(2)}) collective-permute-start(bf16[256,1024]{0,1:T(8,128)(2,1)} %get-tuple-element.34), channel_id=1, source_target_pairs={{0,2},{2,4},{4,6},{6,8},{8,10},{10,12},{12,14},{1,3},{3,5},{5,7},{... | collective-permute-start | bytes 1572872 | tf_op jit(solution)/shard_map/ppermute | solution.py:16
  318.4 6.9 %collective-permute-start.13 = (bf16[256,1024]{0,1:T(8,128)(2,1)}, bf16[256,1024]{0,1:T(8,128)(2,1)S(1)}, u32[]{:S(2)}, u32[]{:S(2)}) collective-permute-start(bf16[256,1024]{0,1:T(8,128)(2,1)} %get-tuple-element.38), channel_id=1, source_target_pairs={{0,6},{2,8},{4,10},{6,12},{8,14},{1,7},{3,9},{5,11},{7,13},{9,15},... | collective-permute-start | bytes 1572872 | tf_op jit(solution)/shard_map/ppermute | solution.py:16
  325.3 5.5 %fusion.44 = f32[1024,2048]{1,0:T(8,128)} fusion(bf16[256,2048]{0,1:T(8,128)(2,1)S(1)} %bitcast.88, bf16[2304,512]{0,1:T(8,128)(2,1)} %bitcast.101, bf16[2304,512]{0,1:T(8,128)(2,1)S(1)} %bitcast.99), kind=kOutput, calls=%fused_computation.67 | convolution fusion | flops 1074790400 | bytes 14155776 | tf_op jit(solution)/shard_map/dot_general | solution.py:20
  332.3 5.6 %fusion.64 = f32[1024,2048]{1,0:T(8,128)} fusion(bf16[256,1024]{0,1:T(8,128)(2,1)} %collective-permute-done.14, bf16[256,2048]{0,1:T(8,128)(2,1)S(1)} %bitcast.89), kind=kOutput, calls=%fused_computation.98 | convolution fusion | flops 1073741824 | bytes 9961472 | tf_op jit(solution)/shard_map/dot_general | solution.py:20
  337.8 3.8 collective-permute-done.13
  342.9 4.5 fusion.63
  347.5 20.4 %collective-permute-start.15 = (bf16[256,1024]{0,1:T(8,128)(2,1)S(1)}, bf16[256,1024]{0,1:T(8,128)(2,1)S(1)}, u32[]{:S(2)}, u32[]{:S(2)}) collective-permute-start(bf16[256,1024]{0,1:T(8,128)(2,1)S(1)} %copy-done.1), channel_id=1, source_target_pairs={{0,8},{2,10},{4,12},{6,14},{1,9},{3,11},{5,13},{7,15},{16,24},{18,... | collective-permute-start | bytes 1572872 | tf_op jit(solution)/shard_map/ppermute | solution.py:16
  367.9 4.5 fusion.62
  372.4 4.5 fusion.61
  376.9 4.5 fusion.60
  381.4 4.5 fusion.59
  385.9 4.5 fusion.58
  390.4 25.2 %add_bitcast_fusion = f32[2048,1024]{0,1:T(8,128)} fusion(f32[1024,2048]{1,0:T(8,128)} %fusion.64, f32[1024,2048]{1,0:T(8,128)} %fusion.63, f32[1024,2048]{1,0:T(8,128)} %fusion.62, f32[1024,2048]{1,0:T(8,128)} %fusion.61, f32[1024,2048]{1,0:T(8,128)} %fusion.60, f32[1024,2048]{1,0:T(8,128)} %fusion.59, f32[1024,2048]{1,0:T(8,128)} %fusion.44, ...), kind=kOutput, calls=%fused_computation.32 | convolution fusion | flops 1090519040 | bytes 77070336 | tf_op jit(solution)/shard_map/dot_general | solution.py:20
  415.7 14.6 %reduce-scatter.3.cloned.1.call-done = f32[1024,1024]{0,1:T(8,128)} async-done(((f32[2048,1024]{0,1:T(8,128)}), f32[1024,1024]{0,1:T(8,128)}) %reduce-scatter.3.cloned.1.call-update) | async-done | bytes 4194320 | tf_op jit(solution)/shard_map/reduce_scatter | solution.py:116
  430.3 93.7 %reduce-scatter.5.cloned.1.call-done = f32[128,1024]{0,1:T(8,128)} async-done(((f32[1024,1024]{0,1:T(8,128)}), f32[128,1024]{0,1:T(8,128)}) %reduce-scatter.5.cloned.1.call-update) | async-done | bytes 524304 | tf_op jit(solution)/shard_map/reduce_scatter | solution.py:117
  524.0 2.0 copy.42
  (63 shorter events, 30.2 us)
Async XLA Ops:
  6.5 423.7 %reduce-scatter.3.cloned.1.call-start = ((), (), s32[]{:S(2)}) async-start(), calls=%async_computation.2 | async-start | bytes 12582912 | tf_op jit(solution)/shard_map/reduce_scatter | solution.py:116
  10.1 194.0 %collective-permute-start.7 = (bf16[1,256,2048]{1,2,0:T(8,128)(2,1)}, bf16[1,256,2048]{1,2,0:T(8,128)(2,1)S(1)}, u32[]{:S(2)}, u32[]{:S(2)}) collective-permute-start(bf16[1,256,2048]{1,2,0:T(8,128)(2,1)} %pad_maximum_fusion), channel_id=1, source_target_pairs={{8,0},{10,2},{12,4},{14,6},{9,1},{11,3},{13,5},{15,7},{24,16},{26,... | collective-permute-start | bytes 3145736 | tf_op jit(solution)/shard_map/ppermute | solution.py:16
  11.4 83.8 %collective-permute-start.3 = (bf16[1,256,2048]{1,2,0:T(8,128)(2,1)}, bf16[1,256,2048]{1,2,0:T(8,128)(2,1)}, u32[]{:S(2)}, u32[]{:S(2)}) collective-permute-start(bf16[1,256,2048]{1,2,0:T(8,128)(2,1)} %pad_maximum_fusion), channel_id=1, source_target_pairs={{0,2},{2,4},{4,6},{6,8},{8,10},{10,12},{12,14},{1,3},{3,5},{5,7},{... | collective-permute-start | bytes 3145736 | tf_op jit(solution)/shard_map/ppermute | solution.py:16
  17.2 75.1 %collective-permute-start.2 = (bf16[1,256,2048]{1,2,0:T(8,128)(2,1)}, bf16[1,256,2048]{1,2,0:T(8,128)(2,1)}, u32[]{:S(2)}, u32[]{:S(2)}) collective-permute-start(bf16[1,256,2048]{1,2,0:T(8,128)(2,1)} %pad_maximum_fusion), channel_id=1, source_target_pairs={{0,4},{2,6},{4,8},{6,10},{8,12},{10,14},{1,5},{3,7},{5,9},{7,11},{... | collective-permute-start | bytes 3145736 | tf_op jit(solution)/shard_map/ppermute | solution.py:16
  20.7 69.0 %collective-permute-start.1 = (bf16[1,256,2048]{1,2,0:T(8,128)(2,1)}, bf16[1,256,2048]{1,2,0:T(8,128)(2,1)}, u32[]{:S(2)}, u32[]{:S(2)}) collective-permute-start(bf16[1,256,2048]{1,2,0:T(8,128)(2,1)} %pad_maximum_fusion), channel_id=1, source_target_pairs={{0,6},{2,8},{4,10},{6,12},{8,14},{1,7},{3,9},{5,11},{7,13},{9,15},... | collective-permute-start | bytes 3145736 | tf_op jit(solution)/shard_map/ppermute | solution.py:16
  26.2 61.0 %collective-permute-start = (bf16[1,256,2048]{1,2,0:T(8,128)(2,1)}, bf16[1,256,2048]{1,2,0:T(8,128)(2,1)}, u32[]{:S(2)}, u32[]{:S(2)}) collective-permute-start(bf16[1,256,2048]{1,2,0:T(8,128)(2,1)} %pad_maximum_fusion), channel_id=1, source_target_pairs={{0,8},{2,10},{4,12},{6,14},{1,9},{3,11},{5,13},{7,15},{16,24},{18,... | collective-permute-start | bytes 3145736 | tf_op jit(solution)/shard_map/ppermute | solution.py:16
  32.1 175.0 %copy-start.4 = (bf16[256,512]{0,1:T(8,128)(2,1)}, bf16[256,512]{0,1:T(8,128)(2,1)S(1)}, u32[]{:S(2)}) copy-start(bf16[256,512]{0,1:T(8,128)(2,1)S(1)} %get-tuple-element.43) | copy-start | bytes 786436
  87.2 45.2 %collective-permute-start.4 = (bf16[1,256,2048]{1,2,0:T(8,128)(2,1)}, bf16[1,256,2048]{1,2,0:T(8,128)(2,1)S(1)}, u32[]{:S(2)}, u32[]{:S(2)}) collective-permute-start(bf16[1,256,2048]{1,2,0:T(8,128)(2,1)} %pad_maximum_fusion), channel_id=1, source_target_pairs={{2,0},{4,2},{6,4},{8,6},{10,8},{12,10},{14,12},{3,1},{5,3},{7,5},{... | collective-permute-start | bytes 3145736 | tf_op jit(solution)/shard_map/ppermute | solution.py:16
  89.8 68.4 %collective-permute-start.5 = (bf16[1,256,2048]{1,2,0:T(8,128)(2,1)}, bf16[1,256,2048]{1,2,0:T(8,128)(2,1)S(1)}, u32[]{:S(2)}, u32[]{:S(2)}) collective-permute-start(bf16[1,256,2048]{1,2,0:T(8,128)(2,1)} %pad_maximum_fusion), channel_id=1, source_target_pairs={{4,0},{6,2},{8,4},{10,6},{12,8},{14,10},{5,1},{7,3},{9,5},{11,7},{... | collective-permute-start | bytes 3145736 | tf_op jit(solution)/shard_map/ppermute | solution.py:16
  92.4 111.6 %collective-permute-start.6 = (bf16[1,256,2048]{1,2,0:T(8,128)(2,1)}, bf16[1,256,2048]{1,2,0:T(8,128)(2,1)S(1)}, u32[]{:S(2)}, u32[]{:S(2)}) collective-permute-start(bf16[1,256,2048]{1,2,0:T(8,128)(2,1)} %pad_maximum_fusion), channel_id=1, source_target_pairs={{6,0},{8,2},{10,4},{12,6},{14,8},{7,1},{9,3},{11,5},{13,7},{15,9},... | collective-permute-start | bytes 3145736 | tf_op jit(solution)/shard_map/ppermute | solution.py:16
  207.2 9.7 %copy-start.7 = (bf16[256,512]{0,1:T(8,128)(2,1)S(1)}, bf16[256,512]{0,1:T(8,128)(2,1)}, u32[]{:S(2)}) copy-start(bf16[256,512]{0,1:T(8,128)(2,1)} %get-tuple-element.44) | copy-start | bytes 786436
  216.8 9.6 %copy-start.8 = (bf16[256,512]{0,1:T(8,128)(2,1)S(1)}, bf16[256,512]{0,1:T(8,128)(2,1)}, u32[]{:S(2)}) copy-start(bf16[256,512]{0,1:T(8,128)(2,1)} %get-tuple-element.42) | copy-start | bytes 786436
  233.4 8.2 %copy-start.6 = (bf16[256,512]{0,1:T(8,128)(2,1)S(1)}, bf16[256,512]{0,1:T(8,128)(2,1)}, u32[]{:S(2)}) copy-start(bf16[256,512]{0,1:T(8,128)(2,1)} %get-tuple-element.41) | copy-start | bytes 786436
  241.6 9.7 %copy-start.5 = (bf16[256,512]{0,1:T(8,128)(2,1)S(1)}, bf16[256,512]{0,1:T(8,128)(2,1)}, u32[]{:S(2)}) copy-start(bf16[256,512]{0,1:T(8,128)(2,1)} %copy-done.4) | copy-start | bytes 786436
  261.5 4.8 copy-start
  265.0 65.9 %collective-permute-start.14 = (bf16[256,1024]{0,1:T(8,128)(2,1)}, bf16[256,1024]{0,1:T(8,128)(2,1)}, u32[]{:S(2)}, u32[]{:S(2)}) collective-permute-start(bf16[256,1024]{0,1:T(8,128)(2,1)} %get-tuple-element.40), channel_id=1, source_target_pairs={{8,0},{10,2},{12,4},{14,6},{9,1},{11,3},{13,5},{15,7},{24,16},{26,... | collective-permute-start | bytes 1572872 | tf_op jit(solution)/shard_map/ppermute | solution.py:16
  268.9 117.0 %collective-permute-start.8 = (bf16[256,1024]{0,1:T(8,128)(2,1)}, bf16[256,1024]{0,1:T(8,128)(2,1)S(1)}, u32[]{:S(2)}, u32[]{:S(2)}) collective-permute-start(bf16[256,1024]{0,1:T(8,128)(2,1)} %get-tuple-element.33), channel_id=1, source_target_pairs={{2,0},{4,2},{6,4},{8,6},{10,8},{12,10},{14,12},{3,1},{5,3},{7,5},{... | collective-permute-start | bytes 1572872 | tf_op jit(solution)/shard_map/ppermute | solution.py:16
  270.2 111.2 %collective-permute-start.9 = (bf16[256,1024]{0,1:T(8,128)(2,1)}, bf16[256,1024]{0,1:T(8,128)(2,1)S(1)}, u32[]{:S(2)}, u32[]{:S(2)}) collective-permute-start(bf16[256,1024]{0,1:T(8,128)(2,1)} %get-tuple-element.34), channel_id=1, source_target_pairs={{0,2},{2,4},{4,6},{6,8},{8,10},{10,12},{12,14},{1,3},{3,5},{5,7},{... | collective-permute-start | bytes 1572872 | tf_op jit(solution)/shard_map/ppermute | solution.py:16
  317.1 59.8 %collective-permute-start.10 = (bf16[256,1024]{0,1:T(8,128)(2,1)}, bf16[256,1024]{0,1:T(8,128)(2,1)S(1)}, u32[]{:S(2)}, u32[]{:S(2)}) collective-permute-start(bf16[256,1024]{0,1:T(8,128)(2,1)} %get-tuple-element.35), channel_id=1, source_target_pairs={{4,0},{6,2},{8,4},{10,6},{12,8},{14,10},{5,1},{7,3},{9,5},{11,7},{... | collective-permute-start | bytes 1572872 | tf_op jit(solution)/shard_map/ppermute | solution.py:16
  318.4 23.3 %collective-permute-start.13 = (bf16[256,1024]{0,1:T(8,128)(2,1)}, bf16[256,1024]{0,1:T(8,128)(2,1)S(1)}, u32[]{:S(2)}, u32[]{:S(2)}) collective-permute-start(bf16[256,1024]{0,1:T(8,128)(2,1)} %get-tuple-element.38), channel_id=1, source_target_pairs={{0,6},{2,8},{4,10},{6,12},{8,14},{1,7},{3,9},{5,11},{7,13},{9,15},... | collective-permute-start | bytes 1572872 | tf_op jit(solution)/shard_map/ppermute | solution.py:16
  325.3 5.5 %copy-start.3 = (bf16[256,1024]{0,1:T(8,128)(2,1)S(1)}, bf16[256,1024]{0,1:T(8,128)(2,1)}, u32[]{:S(2)}) copy-start(bf16[256,1024]{0,1:T(8,128)(2,1)} %get-tuple-element.37) | copy-start | bytes 1572868
  330.8 10.8 %copy-start.2 = (bf16[256,1024]{0,1:T(8,128)(2,1)S(1)}, bf16[256,1024]{0,1:T(8,128)(2,1)}, u32[]{:S(2)}) copy-start(bf16[256,1024]{0,1:T(8,128)(2,1)} %get-tuple-element.36) | copy-start | bytes 1572868
  330.8 16.6 %collective-permute-start.12 = (bf16[256,1024]{0,1:T(8,128)(2,1)S(1)}, bf16[256,1024]{0,1:T(8,128)(2,1)S(1)}, u32[]{:S(2)}, u32[]{:S(2)}) collective-permute-start(bf16[256,1024]{0,1:T(8,128)(2,1)S(1)} %copy-done.3), channel_id=1, source_target_pairs={{6,0},{8,2},{10,4},{12,6},{14,8},{7,1},{9,3},{11,5},{13,7},{15,9},... | collective-permute-start | bytes 1572872 | tf_op jit(solution)/shard_map/ppermute | solution.py:16
  337.8 9.7 %copy-start.1 = (bf16[256,1024]{0,1:T(8,128)(2,1)S(1)}, bf16[256,1024]{0,1:T(8,128)(2,1)}, u32[]{:S(2)}) copy-start(bf16[256,1024]{0,1:T(8,128)(2,1)} %get-tuple-element.39) | copy-start | bytes 1572868
  341.6 30.8 %collective-permute-start.11 = (bf16[256,1024]{0,1:T(8,128)(2,1)S(1)}, bf16[256,1024]{0,1:T(8,128)(2,1)S(1)}, u32[]{:S(2)}, u32[]{:S(2)}) collective-permute-start(bf16[256,1024]{0,1:T(8,128)(2,1)S(1)} %copy-done.2), channel_id=1, source_target_pairs={{0,4},{2,6},{4,8},{6,10},{8,12},{10,14},{1,5},{3,7},{5,9},{7,11},{... | collective-permute-start | bytes 1572872 | tf_op jit(solution)/shard_map/ppermute | solution.py:16
  347.5 42.9 %collective-permute-start.15 = (bf16[256,1024]{0,1:T(8,128)(2,1)S(1)}, bf16[256,1024]{0,1:T(8,128)(2,1)S(1)}, u32[]{:S(2)}, u32[]{:S(2)}) collective-permute-start(bf16[256,1024]{0,1:T(8,128)(2,1)S(1)} %copy-done.1), channel_id=1, source_target_pairs={{0,8},{2,10},{4,12},{6,14},{1,9},{3,11},{5,13},{7,15},{16,24},{18,... | collective-permute-start | bytes 1572872 | tf_op jit(solution)/shard_map/ppermute | solution.py:16
  415.6 108.3 %reduce-scatter.5.cloned.1.call-start = ((), (), s32[]{:S(2)}) async-start(), calls=%async_computation.3 | async-start | bytes 4718592 | tf_op jit(solution)/shard_map/reduce_scatter | solution.py:117
Sparse Core Ops, SparseCore 0:
  415.8 14.4 reduce-scatter.2
  434.3 89.5 reduce-scatter.4
where the time goes:
time: 534 us; the launch traced here: 533 us
  waiting for transfers between devices  272 us (51%)
  matrix products  118 us (22%)
  starting transfers between devices  103 us (19%)
  local copies, waits for them, and re-layouts  19.8 us (4%)
  between operations  13.7 us (3%)
  other arithmetic  6.9 us (1%)
    ppermute x16, waiting for transfers between devices, shifted(): lax.ppermute(value, axis, [(source, source + steps) for source in range(f...  163 us
    ppermute x16, starting transfers between devices, shifted(): lax.ppermute(value, axis, [(source, source + steps) for source in range(f...  103 us
    reduce_scatter x1, waiting for transfers between devices, local(): return lax.psum_scatter(halves, 'seq', scatter_dimension=0, tiled=True)  93.7 us
    dot_general x9, matrix products, dot_rows(): lax.dot_general(left, right, (((0,), (0,)), ((), ())), preferred_element_...  63.3 us
    sub x2, matrix products, window_grads(): weights = jnp.where(visible[None], jnp.exp(scores - row_max), 0.0)  19.3 us
    dot_general x2, matrix products, window_grads(): jnp.einsum('hij,ihe->jhe', dscores.astype(jnp.bfloat16), query_rows, pref...  18.4 us
    dot_general x2, matrix products, window_grads(): jnp.einsum('ihe,jhe->hij', grad_rows, value_rows, preferred_element_type=...  16.6 us
    reduce_scatter x1, waiting for transfers between devices, local(): halves = lax.psum_scatter(result, 'dp', scatter_dimension=0, tiled=True)  14.6 us
  transfers between devices with their start and end apart: 18, of which 7 were waited for; matrix products, arithmetic and copies ran while one was open for 10% of the time, Pallas kernels for 0%

commit v1 on v0

v1 whole, which is shorter than its diff:
```python
import functools
import math

import jax
import jax.numpy as jnp
from jax import lax
from jax.experimental import pallas as pl
from jax.experimental.pallas import tpu as pltpu
from jax.sharding import PartitionSpec as P

HEADS = 8
HEAD_DIM = 128
HALF = 1024
NEG = -1e30
NT = (((1,), (1,)), ((), ()))


def exchange(value, axis, distance):
    count = lax.axis_size(axis)
    return lax.ppermute(value, axis, [(source, source ^ distance) for source in range(count)])


def fold_rows(value, op):
    rows = value.shape[0]
    total = value[0:8]
    for start in range(8, rows, 8):
        total = op(total, value[start : start + 8])
    return total


def head_kernel(tok, halo, groups, place, *refs):
    pieces = refs[0:HEADS]
    refs = refs[HEADS:]
    if halo:
        halves, refs = refs[0:2], refs[2:]
        out_refs, refs = refs[0:1], refs[1:]
    else:
        out_refs, refs = refs[0 : HEADS // 2], refs[HEADS // 2 :]
    query_ref, key_ref, value_ref, grad_ref, score_ref, dprob_ref, total_ref, sem = refs
    me = place[0]
    group_rows = HEADS * tok
    blocks = (group_rows + 2 * halo) // tok
    reach = HALF // tok
    inverse_root = 1.0 / math.sqrt(HEAD_DIM)
    scale = inverse_root * math.log2(math.e)

    copies = []
    for distance in range(HEADS):
        start = pl.multiple_of((me ^ distance) * tok, tok)
        targets = (
            query_ref.at[pl.ds(start, tok)],
            key_ref.at[pl.ds(start + halo, tok)],
            value_ref.at[pl.ds(start + halo, tok)],
            grad_ref.at[pl.ds(start, tok)],
        )
        for index, target in enumerate(targets):
            copies.append(pltpu.make_async_copy(pieces[distance].at[index], target, sem))
    if halo:
        for side, start in ((0, 0), (1, halo + group_rows)):
            for index, target in enumerate((key_ref, value_ref)):
                copies.append(
                    pltpu.make_async_copy(
                        halves[side].at[index], target.at[pl.ds(start, halo)], sem
                    )
                )
    for copy in copies:
        copy.start()
    total_ref[...] = jnp.zeros_like(total_ref)
    for copy in copies:
        copy.wait()

    row = lax.broadcasted_iota(jnp.int32, (tok, tok), 0)
    col = lax.broadcasted_iota(jnp.int32, (tok, tok), 1)
    for b in range(HEADS):
        slot = b % 2
        query = query_ref[b * tok : (b + 1) * tok]
        grad = grad_ref[b * tok : (b + 1) * tok]
        shift = halo // tok
        window = range(max(0, b + shift - reach), min(blocks, b + shift + reach + 1))
        top = None
        for at, kb in enumerate(window):
            key = key_ref[kb * tok : (kb + 1) * tok]
            score = lax.dot_general(key, query, NT, preferred_element_type=jnp.float32)
            if kb - shift == b - reach:
                score = jnp.where(row >= col, score, NEG)
            if kb - shift == b + reach:
                score = jnp.where(row <= col, score, NEG)
            if kb < shift:
                score = jnp.where(place[1] > 0, score, NEG)
            if kb - shift >= HEADS:
                score = jnp.where(place[1] < groups - 1, score, NEG)
            score_ref[slot, at * tok : (at + 1) * tok] = score
            part = fold_rows(score, jnp.maximum)
            top = part if top is None else jnp.maximum(top, part)
        top = jnp.max(top, axis=0, keepdims=True) * scale
        weight_sum = jnp.zeros((8, tok), jnp.float32)
        delta_sum = jnp.zeros((8, tok), jnp.float32)
        for at, kb in enumerate(window):
            value = value_ref[kb * tok : (kb + 1) * tok]
            dprob = lax.dot_general(value, grad, NT, preferred_element_type=jnp.float32)
            weight = jnp.exp2(score_ref[slot, at * tok : (at + 1) * tok] * scale - top)
            score_ref[slot, at * tok : (at + 1) * tok] = weight
            dprob_ref[slot, at * tok : (at + 1) * tok] = dprob
            weight_sum = weight_sum + fold_rows(weight, jnp.add)
            delta_sum = delta_sum + fold_rows(weight * dprob, jnp.add)
        inverse = 1.0 / jnp.sum(weight_sum, axis=0, keepdims=True)
        delta = jnp.sum(delta_sum, axis=0, keepdims=True) * inverse
        for at, kb in enumerate(window):
            prob = score_ref[slot, at * tok : (at + 1) * tok] * inverse
            dscore = prob * (dprob_ref[slot, at * tok : (at + 1) * tok] - delta)
            total_ref[kb * tok : (kb + 1) * tok] += jnp.dot(
                dscore.astype(jnp.bfloat16), query, preferred_element_type=jnp.float32
            )
    if halo:
        out_refs[0][...] = total_ref[...] * inverse_root
    else:
        pair = 2 * tok
        for distance in range(HEADS // 2):
            start = pl.multiple_of(((me // 2) ^ distance) * pair, pair)
            out_refs[distance][...] = (
                total_ref[pl.ds(start, pair)] * inverse_root
            ).astype(jnp.bfloat16)


def head_grads(place, pieces, halves, groups):
    tok = pieces[0].shape[1]
    halo = HALF if halves else 0
    rows = HEADS * tok
    span = rows + 2 * halo
    window = min(span, tok + 2 * HALF)
    if halo:
        out_shape = [jax.ShapeDtypeStruct((span, HEAD_DIM), jnp.float32)]
    else:
        out_shape = [jax.ShapeDtypeStruct((2 * tok, HEAD_DIM), jnp.bfloat16)] * (HEADS // 2)
    any_spec = pl.BlockSpec(memory_space=pl.ANY)
    return pl.pallas_call(
        functools.partial(head_kernel, tok, halo, groups),
        out_shape=out_shape,
        in_specs=[pl.BlockSpec(memory_space=pltpu.SMEM)]
        + [any_spec] * (len(pieces) + len(halves)),
        out_specs=[pl.BlockSpec(memory_space=pltpu.VMEM)] * len(out_shape),
        scratch_shapes=[
            pltpu.VMEM((rows, HEAD_DIM), jnp.bfloat16),
            pltpu.VMEM((span, HEAD_DIM), jnp.bfloat16),
            pltpu.VMEM((span, HEAD_DIM), jnp.bfloat16),
            pltpu.VMEM((rows, HEAD_DIM), jnp.bfloat16),
            pltpu.VMEM((2, window, tok), jnp.float32),
            pltpu.VMEM((2, window, tok), jnp.float32),
            pltpu.VMEM((span, HEAD_DIM), jnp.float32),
            pltpu.SemaphoreType.DMA,
        ],
        compiler_params=pltpu.CompilerParams(vmem_limit_bytes=40 * 2**20),
        cost_estimate=pl.CostEstimate(
            flops=6 * rows * window * HEAD_DIM,
            bytes_accessed=8 * rows * HEAD_DIM,
            transcendentals=rows * window,
        ),
        name="head_grads",
    )(place, *pieces, *halves)


def weight_kernel(place, input_ref, *refs):
    count = HEADS // 2
    own, other = refs[0:count], refs[count : 2 * count]
    out_ref, near_ref, grad_ref = refs[2 * count :]
    column = place[0] // 2
    core = place[2]
    tokens = own[0].shape[0]
    for distance in range(count):
        start = pl.multiple_of((column ^ distance) * HEAD_DIM, HEAD_DIM)
        at = pl.multiple_of(core * tokens, tokens)
        grad_ref[pl.ds(at, tokens), pl.ds(start, HEAD_DIM)] = own[distance][...]
        at = pl.multiple_of((1 - core) * tokens, tokens)
        grad_ref[pl.ds(at, tokens), pl.ds(start, HEAD_DIM)] = other[distance][...]
    for target in range(input_ref.shape[0]):
        product = jnp.dot(
            input_ref[target], grad_ref[...], preferred_element_type=jnp.float32
        )
        out_ref[target] = product.astype(out_ref.dtype)
        if target == 0:
            near_ref[...] = product


def weight_parts(place, inputs, own, other, dtype):
    targets, share, depth = inputs.shape
    width = len(own) * HEAD_DIM
    vmem = pl.BlockSpec(memory_space=pltpu.VMEM)
    return pl.pallas_call(
        weight_kernel,
        out_shape=[
            jax.ShapeDtypeStruct((targets, share, width), dtype),
            jax.ShapeDtypeStruct((share, width), jnp.float32),
        ],
        in_specs=[pl.BlockSpec(memory_space=pltpu.SMEM)] + [vmem] * (1 + len(own) + len(other)),
        out_specs=[vmem, vmem],
        scratch_shapes=[pltpu.VMEM((depth, width), jnp.bfloat16)],
        compiler_params=pltpu.CompilerParams(vmem_limit_bytes=24 * 2**20),
        cost_estimate=pl.CostEstimate(
            flops=2 * targets * share * depth * width,
            bytes_accessed=2 * depth * (width + targets * share),
            transcendentals=0,
        ),
        name="weight_parts",
    )(place, inputs, *own, *other)


def ordered(first, own, other, axis):
    return jnp.where(first == 0, jnp.stack([own, other], axis), jnp.stack([other, own], axis))


def gathered_inputs(layer_input, me, parity, core, groups):
    tok, width = layer_input.shape
    columns = lax.axis_size("seq") // 2
    share = width // (columns * 4)
    shaped = layer_input.reshape(tok, columns, 2, 2, share)
    keep = lax.dynamic_index_in_dim(shaped, parity, 2, keepdims=False)
    give = lax.dynamic_index_in_dim(shaped, 1 - parity, 2, keepdims=False)
    both = ordered(parity, keep, exchange(give, "seq", 1), 0)
    both = both.reshape(2 * tok, columns, 2, share)
    keep = lax.dynamic_index_in_dim(both, core, 2, keepdims=False)
    give = lax.dynamic_index_in_dim(both, 1 - core, 2, keepdims=False)
    full = ordered(core, keep, exchange(give, "dp", 1), 0)
    full = full.reshape(4 * tok, columns, share).transpose(1, 2, 0)
    if groups == 1:
        here = me // 2
        full = jnp.stack(
            [
                lax.dynamic_index_in_dim(full, here ^ distance, 0, keepdims=False)
                for distance in range(columns)
            ]
        )
    return full


def local(queries, key_states, value_states, out_grad, layer_input):
    seq_count = lax.axis_size("seq")
    groups = seq_count // HEADS
    tok = queries.shape[1]
    index = lax.axis_index("seq")
    core = lax.axis_index("dp")
    me = index % HEADS
    group = index // HEADS
    parity = index % 2
    place = jnp.stack([me, group, core]).astype(jnp.int32)

    def piece(distance):
        start = (me ^ distance) * HEAD_DIM
        return jnp.stack(
            [
                lax.dynamic_slice_in_dim(array[0], start, HEAD_DIM, 1)
                for array in (queries, key_states, value_states, out_grad)
            ]
        )

    pieces = [None] * HEADS
    for distance in (6, 7, 4, 5, 2, 3, 1):
        pieces[distance] = exchange(piece(distance), "seq", distance)
    pieces[0] = piece(0)
    inputs = gathered_inputs(layer_input[0], me, parity, core, groups)

    if groups == 1:
        grads = head_grads(place, pieces, [], groups)
    else:
        ordered_pieces = jnp.stack(pieces)
        rows = jnp.stack(
            [
                lax.dynamic_index_in_dim(ordered_pieces, me ^ block, 0, keepdims=False)
                for block in range(HEADS)
            ]
        )
        rows = rows[:, 1:3].transpose(1, 0, 2, 3).reshape(2, HEADS * tok, HEAD_DIM)
        ahead = [(source, source + HEADS) for source in range(seq_count - HEADS)]
        back = [(source + HEADS, source) for source in range(seq_count - HEADS)]
        before = lax.ppermute(rows[:, -HALF:], "seq", ahead)
        after = lax.ppermute(rows[:, :HALF], "seq", back)
        span = head_grads(place, pieces, [before, after], groups)[0]
        from_after = lax.ppermute(span[:HALF].astype(jnp.bfloat16), "seq", back)
        from_before = lax.ppermute(span[-HALF:].astype(jnp.bfloat16), "seq", ahead)
        inner = span[HALF:-HALF]
        inner = inner.at[-HALF:].add(from_after.astype(jnp.float32))
        inner = inner.at[:HALF].add(from_before.astype(jnp.float32))
        inner = inner.astype(jnp.bfloat16)
        grads = [
            lax.dynamic_slice_in_dim(inner, ((me // 2) ^ distance) * 2 * tok, 2 * tok, 0)
            for distance in range(HEADS // 2)
        ]

    near = [grads[0]] + [None] * (HEADS // 2 - 1)
    for distance in (3, 2, 1):
        near[distance] = exchange(grads[distance], "seq", 2 * distance)

    def reduced(own):
        stacked = jnp.stack(own)
        swapped = exchange(stacked, "dp", 1)
        other = [swapped[distance] for distance in range(HEADS // 2)]
        if groups > 1:
            full = weight_parts(place, inputs, own, other, jnp.float32)[0]
            full = full.reshape(-1, full.shape[2])
            members = [list(range(first, seq_count, 2)) for first in (0, 1)]
            return lax.psum_scatter(
                full, "seq", scatter_dimension=0, axis_index_groups=members, tiled=True
            )
        parts, total = weight_parts(place, inputs, own, other, jnp.bfloat16)
        for distance in (3, 2, 1):
            total = total + exchange(parts[distance], "seq", 2 * distance).astype(jnp.float32)
        return total

    stacked = jnp.stack(near)
    far = exchange(stacked, "seq", 1)
    first = reduced(near)
    second = reduced([far[distance] for distance in range(HEADS // 2)])
    share, width = first.shape
    shape = (share, HEADS // 2, HEAD_DIM)
    result = ordered(parity, first.reshape(shape), second.reshape(shape), 2)
    return result.reshape(share, 2 * width)


def solution(mesh):
    spec = P(("parts", "dp"), "seq", None)
    out_specs = P(("parts", "seq", "dp"), None)
    return jax.shard_map(
        local, mesh=mesh, in_specs=(spec,) * 5, out_specs=out_specs, check_vma=False
    )
```

time: 534 us -> 136 us (0.25)
  waiting for transfers between devices: 272 us -> 50.2 us
  matrix products: 118 us -> 0 us
  starting transfers between devices: 103 us -> 41.5 us
  Pallas kernels: 0 us -> 17 us
  between operations: 13.7 us -> 0.31 us
    ppermute x16 -> x21, waiting for transfers between devices: 163 us -> 50.2 us  [exchange(): lax.ppermute(value, axis, [(source, source ^ distance) for source in rang...]
    reduce_scatter x2 -> x0, waiting for transfers between devices: 108 us -> none  [the longest x1 93.7 us: local(): return lax.psum_scatter(halves, 'seq', scatter_dimension=0, tiled=True)]
    dot_general x13 -> x0, matrix products: 98.3 us -> none  [the longest x9 63.3 us: dot_rows(): lax.dot_general(left, right, (((0,), (0,)), ((), ())), preferred_element_...]
    ppermute x16 -> x21, starting transfers between devices: 103 us -> 41.5 us  [exchange(): lax.ppermute(value, axis, [(source, source ^ distance) for source in rang...]
    sub x2 -> x0, matrix products: 19.3 us -> none  [window_grads(): weights = jnp.where(visible[None], jnp.exp(scores - row_max), 0.0)]
    pallas_call x0 -> x3, Pallas kernels: none -> 17 us  [the longest x1 14.1 us: head_grads(): pl.pallas_call(functools.partial(head_kernel, tok, halo, groups), out_sha...]
    unnamed x30 -> x22, local copies, waits for them, and re-layouts: 11.8 us -> 2.82 us
    another operation x1 -> x11, other arithmetic: 0.66 us -> 6.47 us  [the longest x8 6.19 us: piece(): jnp.stack([lax.dynamic_slice_in_dim(array[0], start, HEAD_DIM, 1) for arr...]
  transfers between devices with their start and end apart: 18 -> 21, of which waited for: 7 -> 7; matrix products, arithmetic and copies ran while one was open for 10% -> 15% of each run, Pallas kernels for 0% -> 13%
where the time goes in v1:
time: 136 us
  waiting for transfers between devices  50.2 us (37%)
  starting transfers between devices  41.5 us (31%)
  local copies, waits for them, and re-layouts  18.5 us (14%)
  Pallas kernels  17 us (12%)
  other arithmetic  8.27 us (6%)
    ppermute x21, waiting for transfers between devices, exchange(): lax.ppermute(value, axis, [(source, source ^ distance) for source in rang...  50.2 us
    ppermute x21, starting transfers between devices, exchange(): lax.ppermute(value, axis, [(source, source ^ distance) for source in rang...  41.5 us
    pallas_call x1, Pallas kernels, head_grads(): pl.pallas_call(functools.partial(head_kernel, tok, halo, groups), out_sha...  14.1 us
    another operation x8, other arithmetic, piece(): jnp.stack([lax.dynamic_slice_in_dim(array[0], start, HEAD_DIM, 1) for arr...  6.19 us
    select_n x5, local copies, waits for them, and re-layouts, ordered(): jnp.where(first == 0, jnp.stack([own, other], axis), jnp.stack([other, ow...  5.72 us
    dynamic_slice x2, local copies, waits for them, and re-layouts, piece(): lax.dynamic_slice_in_dim(array[0], start, HEAD_DIM, 1)  3.09 us
    pallas_call x2, Pallas kernels, weight_parts(): pl.pallas_call(weight_kernel, out_shape=[jax.ShapeDtypeStruct((targets, s...  2.92 us
    unnamed x22, local copies, waits for them, and re-layouts  2.82 us
  transfers between devices with their start and end apart: 21, of which 7 were waited for; matrix products, arithmetic and copies ran while one was open for 15% of the time, Pallas kernels for 13%

profile of v1, /device:TPU:0, one launch (start us, length us, event | category | flops | bytes accessed | tf_op | source)
XLA Modules:
  0.0 135.7 jit_solution(8200680171175370023)
XLA Ops:
  0.0 2.1 %constant_dynamic-slice_fusion.2 = (bf16[1,256,128]{2,1,0:T(8,128)(2,1)}, bf16[1,256,128]{2,1,0:T(8,128)(2,1)S(1)}, bf16[1,256,128]{2,1,0:T(8,128)(2,1)S(1)}, bf...) fusion(bf16[1,256,1024]{2,1,0:T(8,128)(2,1)} %param.6, ...), kind=kLoop, calls=%fused_computation.43 | loop fusion | bytes 2097184 | tf_op jit(solution)/shard_map/dynamic_slice | solution.py:250
  3.8 3.0 %collective-permute-start.2 = (bf16[4,256,128]{2,1,0:T(8,128)(2,1)}, bf16[4,256,128]{2,1,0:T(8,128)(2,1)S(1)}, u32[]{:S(2)}, u32[]{:S(2)}) collective-permute-start(bf16[4,256,128]{2,1,0:T(8,128)(2,1)} %pad_maximum_fusion.3), channel_id=1, source_target_pairs={{0,2},{2,0},{4,6},{6,4},{8,10},{10,8},{12,14},{14,12},{1,3},{3,1},... | collective-permute-start | bytes 786440 | tf_op jit(solution)/shard_map/ppermute | solution.py:20
  7.6 1.6 %collective-permute-start.3 = (bf16[4,256,128]{2,1,0:T(8,128)(2,1)}, bf16[4,256,128]{2,1,0:T(8,128)(2,1)S(1)}, u32[]{:S(2)}, u32[]{:S(2)}) collective-permute-start(bf16[4,256,128]{2,1,0:T(8,128)(2,1)} %pad_maximum_fusion.4), channel_id=1, source_target_pairs={{0,4},{2,6},{4,0},{6,2},{8,12},{10,14},{12,8},{14,10},{1,5},{3,7},... | collective-permute-start | bytes 786440 | tf_op jit(solution)/shard_map/ppermute | solution.py:20
  10.6 3.0 %collective-permute-start.5 = (bf16[4,256,128]{2,1,0:T(8,128)(2,1)}, bf16[4,256,128]{2,1,0:T(8,128)(2,1)S(1)}, u32[]{:S(2)}, u32[]{:S(2)}) collective-permute-start(bf16[4,256,128]{2,1,0:T(8,128)(2,1)} %pad_maximum_fusion.6), channel_id=1, source_target_pairs={{0,8},{2,10},{4,12},{6,14},{8,0},{10,2},{12,4},{14,6},{1,9},{3,11}... | collective-permute-start | bytes 786440 | tf_op jit(solution)/shard_map/ppermute | solution.py:20
  14.3 1.3 collective-permute-start.6
  16.4 1.7 %pad_maximum_fusion.8 = bf16[4,256,128]{2,1,0:T(8,128)(2,1)} fusion(bf16[1,256,128]{2,1,0:T(8,128)(2,1)} %get-tuple-element.78, bf16[1,256,128]{2,1,0:T(8,128)(2,1)} %get-tuple-element.79, bf16[1,256,128]{2,1,0:T(8,128)(2,1)} %get-tuple-element.62, bf16[1,256,128]{2,1,0:T(8,128)(2,1)} %get-tuple-element.87), kind=kLoop, calls=%fused_computation.15 | loop fusion | flops 393216 | bytes 524288 | tf_op jit(solution)/shard_map/stack | solution.py:248
  18.9 3.6 %collective-permute-start.7 = (bf16[4,256,128]{2,1,0:T(8,128)(2,1)}, bf16[4,256,128]{2,1,0:T(8,128)(2,1)S(1)}, u32[]{:S(2)}, u32[]{:S(2)}) collective-permute-start(bf16[4,256,128]{2,1,0:T(8,128)(2,1)} %pad_maximum_fusion.8), channel_id=1, source_target_pairs={{0,12},{2,14},{4,8},{6,10},{8,4},{10,6},{12,0},{14,2},{1,13},{3,15... | collective-permute-start | bytes 786440 | tf_op jit(solution)/shard_map/ppermute | solution.py:20
  22.5 4.1 %collective-permute-done.3.refs_2_ = bf16[4,256,128]{2,1,0:T(8,128)(2,1)S(1)} collective-permute-done((bf16[4,256,128]{2,1,0:T(8,128)(2,1)}, bf16[4,256,128]{2,1,0:T(8,128)(2,1)S(1)}, u32[]{:S(2)}, u32[]{:S(2)}) %collective-permute-start.3) | collective-permute-done | bytes 262176 | tf_op jit(solution)/shard_map/ppermute | solution.py:20
  26.8 1.5 %constant_dynamic-slice_fusion.33 = (bf16[256,4,1,2,128]{4,3,2,1,0:T(2,128)(2,1)S(1)}, bf16[256,4,1,2,128]{4,3,2,1,0:T(2,128)(2,1)}) fusion(bf16[256,4,2,2,128]{4,3,2,1,0:T(2,128)(2,1)S(1)} %reshape_squeeze.3, s32[]{:T(128)S(6)} %select_n.135, s32[]{:T(128)S(6)} %select_n.136), kind=kLoop, calls=%fused_computation.74 | loop fusion | bytes 2097160 | tf_op jit(solution)/shard_map/jit(dynamic_index_in_dim)/dynamic_slice | solution.py:216
  28.3 1.9 %copy.23 = bf16[256,4,1,2,128]{4,0,3,1,2:T(8,128)(2,1)} copy(bf16[256,4,1,2,128]{4,3,2,1,0:T(2,128)(2,1)} %get-tuple-element.28) | data formatting | bytes 1048576
  30.4 2.6 %collective-permute-start = (bf16[256,4,2,128]{3,0,2,1:T(8,128)(2,1)}, bf16[256,4,2,128]{3,0,2,1:T(8,128)(2,1)S(1)}, u32[]{:S(2)}, u32[]{:S(2)}) collective-permute-start(bf16[256,4,2,128]{3,0,2,1:T(8,128)(2,1)} %bitcast.64), channel_id=1, source_target_pairs={{0,2},{2,0},{4,6},{6,4},{8,10},{10,8},{12,14},{14,12},{1,3},{3,1},... | collective-permute-start | bytes 1572872 | tf_op jit(solution)/shard_map/ppermute | solution.py:20
  33.0 17.4 %collective-permute-done.6.refs_5_ = bf16[4,256,128]{2,1,0:T(8,128)(2,1)S(1)} collective-permute-done((bf16[4,256,128]{2,1,0:T(8,128)(2,1)}, bf16[4,256,128]{2,1,0:T(8,128)(2,1)S(1)}, u32[]{:S(2)}, u32[]{:S(2)}) %collective-permute-start.6) | collective-permute-done | bytes 262176 | tf_op jit(solution)/shard_map/ppermute | solution.py:20
  50.4 14.1 %head_grads.1 = (bf16[512,128]{1,0:T(8,128)(2,1)S(1)}, bf16[512,128]{1,0:T(8,128)(2,1)S(1)}, bf16[512,128]{1,0:T(8,128)(2,1)S(1)}, bf16[512,128]{1,0:T(8,128)(2,1)S(1)}) custom-call(s32[3]{0:T(128)S(1)} %pad_add_fusion.place, bf16[4,256,128]{2,1,0:T(8,128)(2,1)S(1)} %pad_maximum_fusion.2.refs_0_, bf16[4,256,128]{2,1,0:T(8,128)(2,1)S(1)} %collective-permute-done.2.refs_1_, ...), custom_call_target="tpu_custom_call" | custom-call | flops 3221225472 | bytes 2097152 | tf_op jit(solution)/shard_map/head_grads/pallas_call | solution.py:136
  64.5 9.9 %collective-permute-start.9 = (bf16[512,128]{1,0:T(8,128)(2,1)S(1)}, bf16[512,128]{1,0:T(8,128)(2,1)S(1)}, u32[]{:S(2)}, u32[]{:S(2)}) collective-permute-start(bf16[512,128]{1,0:T(8,128)(2,1)S(1)} %get-tuple-element.14), channel_id=1, source_target_pairs={{0,4},{2,6},{4,0},{6,2},{8,12},{10,14},{12,8},{14,10},{1,5},{3,7},... | collective-permute-start | bytes 393224 | tf_op jit(solution)/shard_map/ppermute | solution.py:20
  74.4 2.2 %collective-permute-start.10 = (bf16[512,128]{1,0:T(8,128)(2,1)S(1)}, bf16[512,128]{1,0:T(8,128)(2,1)S(1)}, u32[]{:S(2)}, u32[]{:S(2)}) collective-permute-start(bf16[512,128]{1,0:T(8,128)(2,1)S(1)} %get-tuple-element.15), channel_id=1, source_target_pairs={{0,8},{2,10},{4,12},{6,14},{8,0},{10,2},{12,4},{14,6},{1,9},{3,11}... | collective-permute-start | bytes 393224 | tf_op jit(solution)/shard_map/ppermute | solution.py:20
  76.6 1.4 %collective-permute-start.11 = (bf16[512,128]{1,0:T(8,128)(2,1)S(1)}, bf16[512,128]{1,0:T(8,128)(2,1)S(1)}, u32[]{:S(2)}, u32[]{:S(2)}) collective-permute-start(bf16[512,128]{1,0:T(8,128)(2,1)S(1)} %get-tuple-element.16), channel_id=1, source_target_pairs={{0,12},{2,14},{4,8},{6,10},{8,4},{10,6},{12,0},{14,2},{1,13},{3,15... | collective-permute-start | bytes 393224 | tf_op jit(solution)/shard_map/ppermute | solution.py:20
  78.5 8.0 %collective-permute-done.10.refs_2_ = bf16[512,128]{1,0:T(8,128)(2,1)S(1)} collective-permute-done((bf16[512,128]{1,0:T(8,128)(2,1)S(1)}, bf16[512,128]{1,0:T(8,128)(2,1)S(1)}, u32[]{:S(2)}, u32[]{:S(2)}) %collective-permute-start.10) | collective-permute-done | bytes 131104 | tf_op jit(solution)/shard_map/ppermute | solution.py:20
  89.0 7.1 %collective-permute-done.16 = bf16[4,512,128]{2,1,0:T(8,128)(2,1)} collective-permute-done((bf16[4,512,128]{2,1,0:T(8,128)(2,1)S(1)}, bf16[4,512,128]{2,1,0:T(8,128)(2,1)}, u32[]{:S(2)}, u32[]{:S(2)}) %collective-permute-start.16) | collective-permute-done | bytes 524320 | tf_op jit(solution)/shard_map/ppermute | solution.py:20
  96.1 1.1 slice_bitcast_fusion.4
  97.2 1.1 slice_bitcast_fusion.8
  99.2 1.4 %maximum_select_fusion.1 = bf16[2,512,4,128]{3,1,2,0:T(8,128)(2,1)S(1)} fusion(bf16[1,512,4,128]{3,1,2,0:T(8,128)(2,1)} %bitcast.72, bf16[1,512,4,128]{3,1,2,0:T(8,128)(2,1)S(1)} %get-tuple-element.25, pred[]{:T(512)S(6)} %eq.11), kind=kLoop, calls=%fused_computation.1 | loop fusion | flops 1572864 | bytes 2097153 | tf_op jit(solution)/shard_map/jit(_where)/select_n | solution.py:208
  100.6 2.2 %copy.17 = bf16[2,512,4,128]{1,0,3,2:T(2,128)(2,1)} copy(bf16[2,512,4,128]{3,1,2,0:T(8,128)(2,1)S(1)} %maximum_select_fusion.1) | data formatting | bytes 2097152 | tf_op jit(solution)/shard_map/jit(_where)/select_n | solution.py:208
  102.8 1.8 %select_n.142 = bf16[1024,4,128]{0,2,1:T(8,128)(2,1)S(1)} reshape(bf16[2,512,4,128]{1,0,3,2:T(2,128)(2,1)} %copy.17) | data formatting | bytes 2097152 | tf_op jit(solution)/shard_map/jit(_where)/select_n | solution.py:208
  104.8 1.5 %weight_parts.2 = (bf16[4,128,512]{2,1,0:T(8,128)(2,1)S(1)}, f32[128,512]{1,0:T(8,128)S(1)}) custom-call(s32[3]{0:T(128)S(1)} %pad_add_fusion.place, bf16[4,128,1024]{2,1,0:T(8,128)(2,1)S(1)} %pad_maximum_fusion.input_ref, bf16[512,128]{1,0:T(8,128)(2,1)S(1)} %get-tuple-element.13.refs_0_, bf16[512,128]{1,0:T(8,128)(2,1)S(1)} %collective-permute-done.9.refs_1_, ...), custom_call_target="tpu_custom_call" | custom-call | flops 536870912 | bytes 2097152 | tf_op jit(solution)/shard_map/weight_parts/pallas_call | solution.py:188
  106.3 3.4 %collective-permute-start.13 = (bf16[128,512]{1,0:T(8,128)(2,1)S(1)}, bf16[128,512]{1,0:T(8,128)(2,1)S(1)}, u32[]{:S(2)}, u32[]{:S(2)}) collective-permute-start(bf16[128,512]{1,0:T(8,128)(2,1)S(1)} %get-tuple-element.29), channel_id=1, source_target_pairs={{0,12},{2,14},{4,8},{6,10},{8,4},{10,6},{12,0},{14,2},{1,13},{3,15... | collective-permute-start | bytes 393224 | tf_op jit(solution)/shard_map/ppermute | solution.py:20
  109.7 3.0 %collective-permute-start.14 = (bf16[128,512]{1,0:T(8,128)(2,1)S(1)}, bf16[128,512]{1,0:T(8,128)(2,1)S(1)}, u32[]{:S(2)}, u32[]{:S(2)}) collective-permute-start(bf16[128,512]{1,0:T(8,128)(2,1)S(1)} %get-tuple-element.31), channel_id=1, source_target_pairs={{0,8},{2,10},{4,12},{6,14},{8,0},{10,2},{12,4},{14,6},{1,9},{3,11}... | collective-permute-start | bytes 393224 | tf_op jit(solution)/shard_map/ppermute | solution.py:20
  113.9 1.5 %weight_parts.3 = (bf16[4,128,512]{2,1,0:T(8,128)(2,1)S(1)}, f32[128,512]{1,0:T(8,128)S(1)}) custom-call(s32[3]{0:T(128)S(1)} %pad_add_fusion.place, bf16[4,128,1024]{2,1,0:T(8,128)(2,1)S(1)} %pad_maximum_fusion.input_ref, bf16[512,128]{1,0:T(8,128)(2,1)S(1)} %get-tuple-element.46.refs_0_, bf16[512,128]{1,0:T(8,128)(2,1)S(1)} %get-tuple-element.45.refs_1_, ...), custom_call_target="tpu_custom_call" | custom-call | flops 536870912 | bytes 2097152 | tf_op jit(solution)/shard_map/weight_parts/pallas_call | solution.py:188
  115.4 2.4 %collective-permute-start.18 = (bf16[128,512]{1,0:T(8,128)(2,1)S(1)}, bf16[128,512]{1,0:T(8,128)(2,1)S(1)}, u32[]{:S(2)}, u32[]{:S(2)}) collective-permute-start(bf16[128,512]{1,0:T(8,128)(2,1)S(1)} %get-tuple-element.36), channel_id=1, source_target_pairs={{0,12},{2,14},{4,8},{6,10},{8,4},{10,6},{12,0},{14,2},{1,13},{3,15... | collective-permute-start | bytes 393224 | tf_op jit(solution)/shard_map/ppermute | solution.py:20
  118.9 1.7 %collective-permute-start.20 = (bf16[128,512]{1,0:T(8,128)(2,1)S(1)}, bf16[128,512]{1,0:T(8,128)(2,1)S(1)}, u32[]{:S(2)}, u32[]{:S(2)}) collective-permute-start(bf16[128,512]{1,0:T(8,128)(2,1)S(1)} %get-tuple-element.37), channel_id=1, source_target_pairs={{0,4},{2,6},{4,0},{6,2},{8,12},{10,14},{12,8},{14,10},{1,5},{3,7},... | collective-permute-start | bytes 393224 | tf_op jit(solution)/shard_map/ppermute | solution.py:20
  120.6 7.7 %collective-permute-done.14 = bf16[128,512]{1,0:T(8,128)(2,1)S(1)} collective-permute-done((bf16[128,512]{1,0:T(8,128)(2,1)S(1)}, bf16[128,512]{1,0:T(8,128)(2,1)S(1)}, u32[]{:S(2)}, u32[]{:S(2)}) %collective-permute-start.14) | collective-permute-done | bytes 131104 | tf_op jit(solution)/shard_map/ppermute | solution.py:20
  128.5 5.3 %collective-permute-done.19 = bf16[128,512]{1,0:T(8,128)(2,1)S(1)} collective-permute-done((bf16[128,512]{1,0:T(8,128)(2,1)S(1)}, bf16[128,512]{1,0:T(8,128)(2,1)S(1)}, u32[]{:S(2)}, u32[]{:S(2)}) %collective-permute-start.19) | collective-permute-done | bytes 131104 | tf_op jit(solution)/shard_map/ppermute | solution.py:20
  134.5 1.2 select_n.157
  (69 shorter events, 13.7 us)
Async XLA Ops:
  0.0 2.1 %copy-start.2 = (bf16[1,256,1024]{2,1,0:T(8,128)(2,1)S(1)}, bf16[1,256,1024]{2,1,0:T(8,128)(2,1)}, u32[]{:S(2)}) copy-start(bf16[1,256,1024]{2,1,0:T(8,128)(2,1)} %param.8) | copy-start | bytes 1572868
  0.0 2.1 %copy-start.3 = (bf16[1,256,1024]{2,1,0:T(8,128)(2,1)S(1)}, bf16[1,256,1024]{2,1,0:T(8,128)(2,1)}, u32[]{:S(2)}) copy-start(bf16[1,256,1024]{2,1,0:T(8,128)(2,1)} %param.7) | copy-start | bytes 1572868
  3.8 15.1 %collective-permute-start.2 = (bf16[4,256,128]{2,1,0:T(8,128)(2,1)}, bf16[4,256,128]{2,1,0:T(8,128)(2,1)S(1)}, u32[]{:S(2)}, u32[]{:S(2)}) collective-permute-start(bf16[4,256,128]{2,1,0:T(8,128)(2,1)} %pad_maximum_fusion.3), channel_id=1, source_target_pairs={{0,2},{2,0},{4,6},{6,4},{8,10},{10,8},{12,14},{14,12},{1,3},{3,1},... | collective-permute-start | bytes 786440 | tf_op jit(solution)/shard_map/ppermute | solution.py:20
  6.8 8.8 %copy-start = (bf16[1,256,2048]{2,1,0:T(8,128)(2,1)S(1)}, bf16[1,256,2048]{2,1,0:T(8,128)(2,1)}, u32[]{:S(2)}) copy-start(bf16[1,256,2048]{2,1,0:T(8,128)(2,1)} %param.9) | copy-start | bytes 3145732
  7.6 19.0 %collective-permute-start.3 = (bf16[4,256,128]{2,1,0:T(8,128)(2,1)}, bf16[4,256,128]{2,1,0:T(8,128)(2,1)S(1)}, u32[]{:S(2)}, u32[]{:S(2)}) collective-permute-start(bf16[4,256,128]{2,1,0:T(8,128)(2,1)} %pad_maximum_fusion.4), channel_id=1, source_target_pairs={{0,4},{2,6},{4,0},{6,2},{8,12},{10,14},{12,8},{14,10},{1,5},{3,7},... | collective-permute-start | bytes 786440 | tf_op jit(solution)/shard_map/ppermute | solution.py:20
  9.9 20.5 %collective-permute-start.4 = (bf16[4,256,128]{2,1,0:T(8,128)(2,1)}, bf16[4,256,128]{2,1,0:T(8,128)(2,1)S(1)}, u32[]{:S(2)}, u32[]{:S(2)}) collective-permute-start(bf16[4,256,128]{2,1,0:T(8,128)(2,1)} %pad_maximum_fusion.5), channel_id=1, source_target_pairs={{0,6},{2,4},{4,2},{6,0},{8,14},{10,12},{12,10},{14,8},{1,7},{3,5},... | collective-permute-start | bytes 786440 | tf_op jit(solution)/shard_map/ppermute | solution.py:20
  10.6 22.4 %collective-permute-start.5 = (bf16[4,256,128]{2,1,0:T(8,128)(2,1)}, bf16[4,256,128]{2,1,0:T(8,128)(2,1)S(1)}, u32[]{:S(2)}, u32[]{:S(2)}) collective-permute-start(bf16[4,256,128]{2,1,0:T(8,128)(2,1)} %pad_maximum_fusion.6), channel_id=1, source_target_pairs={{0,8},{2,10},{4,12},{6,14},{8,0},{10,2},{12,4},{14,6},{1,9},{3,11}... | collective-permute-start | bytes 786440 | tf_op jit(solution)/shard_map/ppermute | solution.py:20
  14.3 36.1 %collective-permute-start.6 = (bf16[4,256,128]{2,1,0:T(8,128)(2,1)}, bf16[4,256,128]{2,1,0:T(8,128)(2,1)S(1)}, u32[]{:S(2)}, u32[]{:S(2)}) collective-permute-start(bf16[4,256,128]{2,1,0:T(8,128)(2,1)} %pad_maximum_fusion.7), channel_id=1, source_target_pairs={{0,10},{2,8},{4,14},{6,12},{8,2},{10,0},{12,6},{14,4},{1,11},{3,9}... | collective-permute-start | bytes 786440 | tf_op jit(solution)/shard_map/ppermute | solution.py:20
  16.4 1.8 %copy-start.6 = (bf16[1,256,128]{2,1,0:T(8,128)(2,1)S(1)}, bf16[1,256,128]{2,1,0:T(8,128)(2,1)}, u32[]{:S(2)}) copy-start(bf16[1,256,128]{2,1,0:T(8,128)(2,1)} %get-tuple-element.55) | copy-start | bytes 196612
  16.4 1.8 %copy-start.7 = (bf16[1,256,128]{2,1,0:T(8,128)(2,1)S(1)}, bf16[1,256,128]{2,1,0:T(8,128)(2,1)}, u32[]{:S(2)}) copy-start(bf16[1,256,128]{2,1,0:T(8,128)(2,1)} %get-tuple-element.94) | copy-start | bytes 196612
  16.4 1.8 %copy-start.8 = (bf16[1,256,128]{2,1,0:T(8,128)(2,1)S(1)}, bf16[1,256,128]{2,1,0:T(8,128)(2,1)}, u32[]{:S(2)}) copy-start(bf16[1,256,128]{2,1,0:T(8,128)(2,1)} %get-tuple-element.71) | copy-start | bytes 196612
  16.4 1.8 %copy-start.9 = (bf16[1,256,128]{2,1,0:T(8,128)(2,1)S(1)}, bf16[1,256,128]{2,1,0:T(8,128)(2,1)}, u32[]{:S(2)}) copy-start(bf16[1,256,128]{2,1,0:T(8,128)(2,1)} %get-tuple-element.86) | copy-start | bytes 196612
  18.9 31.5 %collective-permute-start.7 = (bf16[4,256,128]{2,1,0:T(8,128)(2,1)}, bf16[4,256,128]{2,1,0:T(8,128)(2,1)S(1)}, u32[]{:S(2)}, u32[]{:S(2)}) collective-permute-start(bf16[4,256,128]{2,1,0:T(8,128)(2,1)} %pad_maximum_fusion.8), channel_id=1, source_target_pairs={{0,12},{2,14},{4,8},{6,10},{8,4},{10,6},{12,0},{14,2},{1,13},{3,15... | collective-permute-start | bytes 786440 | tf_op jit(solution)/shard_map/ppermute | solution.py:20
  26.6 23.8 %collective-permute-start.8 = (bf16[4,256,128]{2,1,0:T(8,128)(2,1)}, bf16[4,256,128]{2,1,0:T(8,128)(2,1)S(1)}, u32[]{:S(2)}, u32[]{:S(2)}) collective-permute-start(bf16[4,256,128]{2,1,0:T(8,128)(2,1)} %pad_maximum_fusion.9), channel_id=1, source_target_pairs={{0,14},{2,12},{4,10},{6,8},{8,6},{10,4},{12,2},{14,0},{1,15},{3,13... | collective-permute-start | bytes 786440 | tf_op jit(solution)/shard_map/ppermute | solution.py:20
  28.3 2.0 %copy-start.4 = (bf16[1,256,128]{2,1,0:T(8,128)(2,1)S(1)}, bf16[1,256,128]{2,1,0:T(8,128)(2,1)}, u32[]{:S(2)}) copy-start(bf16[1,256,128]{2,1,0:T(8,128)(2,1)} %get-tuple-element.77) | copy-start | bytes 196612
  28.3 2.0 %copy-start.5 = (bf16[1,256,128]{2,1,0:T(8,128)(2,1)S(1)}, bf16[1,256,128]{2,1,0:T(8,128)(2,1)}, u32[]{:S(2)}) copy-start(bf16[1,256,128]{2,1,0:T(8,128)(2,1)} %get-tuple-element.80) | copy-start | bytes 196612
  30.4 56.9 %collective-permute-start = (bf16[256,4,2,128]{3,0,2,1:T(8,128)(2,1)}, bf16[256,4,2,128]{3,0,2,1:T(8,128)(2,1)S(1)}, u32[]{:S(2)}, u32[]{:S(2)}) collective-permute-start(bf16[256,4,2,128]{3,0,2,1:T(8,128)(2,1)} %bitcast.64), channel_id=1, source_target_pairs={{0,2},{2,0},{4,6},{6,4},{8,10},{10,8},{12,14},{14,12},{1,3},{3,1},... | collective-permute-start | bytes 1572872 | tf_op jit(solution)/shard_map/ppermute | solution.py:20
  64.5 14.0 %collective-permute-start.9 = (bf16[512,128]{1,0:T(8,128)(2,1)S(1)}, bf16[512,128]{1,0:T(8,128)(2,1)S(1)}, u32[]{:S(2)}, u32[]{:S(2)}) collective-permute-start(bf16[512,128]{1,0:T(8,128)(2,1)S(1)} %get-tuple-element.14), channel_id=1, source_target_pairs={{0,4},{2,6},{4,0},{6,2},{8,12},{10,14},{12,8},{14,10},{1,5},{3,7},... | collective-permute-start | bytes 393224 | tf_op jit(solution)/shard_map/ppermute | solution.py:20
  74.4 12.1 %collective-permute-start.10 = (bf16[512,128]{1,0:T(8,128)(2,1)S(1)}, bf16[512,128]{1,0:T(8,128)(2,1)S(1)}, u32[]{:S(2)}, u32[]{:S(2)}) collective-permute-start(bf16[512,128]{1,0:T(8,128)(2,1)S(1)} %get-tuple-element.15), channel_id=1, source_target_pairs={{0,8},{2,10},{4,12},{6,14},{8,0},{10,2},{12,4},{14,6},{1,9},{3,11}... | collective-permute-start | bytes 393224 | tf_op jit(solution)/shard_map/ppermute | solution.py:20
  76.6 9.9 %collective-permute-start.11 = (bf16[512,128]{1,0:T(8,128)(2,1)S(1)}, bf16[512,128]{1,0:T(8,128)(2,1)S(1)}, u32[]{:S(2)}, u32[]{:S(2)}) collective-permute-start(bf16[512,128]{1,0:T(8,128)(2,1)S(1)} %get-tuple-element.16), channel_id=1, source_target_pairs={{0,12},{2,14},{4,8},{6,10},{8,4},{10,6},{12,0},{14,2},{1,13},{3,15... | collective-permute-start | bytes 393224 | tf_op jit(solution)/shard_map/ppermute | solution.py:20
  86.6 9.5 %collective-permute-start.16 = (bf16[4,512,128]{2,1,0:T(8,128)(2,1)S(1)}, bf16[4,512,128]{2,1,0:T(8,128)(2,1)}, u32[]{:S(2)}, u32[]{:S(2)}) collective-permute-start(bf16[4,512,128]{2,1,0:T(8,128)(2,1)S(1)} %pad_maximum_fusion.1), channel_id=1, source_target_pairs={{0,2},{2,0},{4,6},{6,4},{8,10},{10,8},{12,14},{14,12},{1,3},{3,1},... | collective-permute-start | bytes 1572872 | tf_op jit(solution)/shard_map/ppermute | solution.py:20
  87.3 10.0 %collective-permute-start.12 = (bf16[4,512,128]{2,1,0:T(8,128)(2,1)S(1)}, bf16[4,512,128]{2,1,0:T(8,128)(2,1)}, u32[]{:S(2)}, u32[]{:S(2)}) collective-permute-start(bf16[4,512,128]{2,1,0:T(8,128)(2,1)S(1)} %pad_maximum_fusion.1), channel_id=1, source_target_pairs={{0,1},{1,0},{2,3},{3,2},{4,5},{5,4},{6,7},{7,6},{8,9},{9,8},{10,11... | collective-permute-start | bytes 1572872 | tf_op jit(solution)/shard_map/ppermute | solution.py:20
  88.5 9.9 %collective-permute-start.1 = (bf16[512,4,128]{2,0,1:T(8,128)(2,1)}, bf16[512,4,128]{2,0,1:T(8,128)(2,1)S(1)}, u32[]{:S(2)}, u32[]{:S(2)}) collective-permute-start(bf16[512,4,128]{2,0,1:T(8,128)(2,1)} %get-tuple-element.26), channel_id=1, source_target_pairs={{0,1},{1,0},{2,3},{3,2},{4,5},{5,4},{6,7},{7,6},{8,9},{9,8},{10,11... | collective-permute-start | bytes 1572872 | tf_op jit(solution)/shard_map/ppermute | solution.py:20
  96.1 16.7 %collective-permute-start.17 = (bf16[4,512,128]{2,1,0:T(8,128)(2,1)}, bf16[4,512,128]{2,1,0:T(8,128)(2,1)}, u32[]{:S(2)}, u32[]{:S(2)}) collective-permute-start(bf16[4,512,128]{2,1,0:T(8,128)(2,1)} %collective-permute-done.16), channel_id=1, source_target_pairs={{0,1},{1,0},{2,3},{3,2},{4,5},{5,4},{6,7},{7,6},{8,9},{9,8},{10,11... | collective-permute-start | bytes 1572872 | tf_op jit(solution)/shard_map/ppermute | solution.py:20
  98.4 0.8 copy-start.1
  106.3 12.6 %collective-permute-start.13 = (bf16[128,512]{1,0:T(8,128)(2,1)S(1)}, bf16[128,512]{1,0:T(8,128)(2,1)S(1)}, u32[]{:S(2)}, u32[]{:S(2)}) collective-permute-start(bf16[128,512]{1,0:T(8,128)(2,1)S(1)} %get-tuple-element.29), channel_id=1, source_target_pairs={{0,12},{2,14},{4,8},{6,10},{8,4},{10,6},{12,0},{14,2},{1,13},{3,15... | collective-permute-start | bytes 393224 | tf_op jit(solution)/shard_map/ppermute | solution.py:20
  109.7 18.6 %collective-permute-start.14 = (bf16[128,512]{1,0:T(8,128)(2,1)S(1)}, bf16[128,512]{1,0:T(8,128)(2,1)S(1)}, u32[]{:S(2)}, u32[]{:S(2)}) collective-permute-start(bf16[128,512]{1,0:T(8,128)(2,1)S(1)} %get-tuple-element.31), channel_id=1, source_target_pairs={{0,8},{2,10},{4,12},{6,14},{8,0},{10,2},{12,4},{14,6},{1,9},{3,11}... | collective-permute-start | bytes 393224 | tf_op jit(solution)/shard_map/ppermute | solution.py:20
  112.7 15.6 %collective-permute-start.15 = (bf16[128,512]{1,0:T(8,128)(2,1)S(1)}, bf16[128,512]{1,0:T(8,128)(2,1)S(1)}, u32[]{:S(2)}, u32[]{:S(2)}) collective-permute-start(bf16[128,512]{1,0:T(8,128)(2,1)S(1)} %get-tuple-element.30), channel_id=1, source_target_pairs={{0,4},{2,6},{4,0},{6,2},{8,12},{10,14},{12,8},{14,10},{1,5},{3,7},... | collective-permute-start | bytes 393224 | tf_op jit(solution)/shard_map/ppermute | solution.py:20
  115.4 13.0 %collective-permute-start.18 = (bf16[128,512]{1,0:T(8,128)(2,1)S(1)}, bf16[128,512]{1,0:T(8,128)(2,1)S(1)}, u32[]{:S(2)}, u32[]{:S(2)}) collective-permute-start(bf16[128,512]{1,0:T(8,128)(2,1)S(1)} %get-tuple-element.36), channel_id=1, source_target_pairs={{0,12},{2,14},{4,8},{6,10},{8,4},{10,6},{12,0},{14,2},{1,13},{3,15... | collective-permute-start | bytes 393224 | tf_op jit(solution)/shard_map/ppermute | solution.py:20
  117.9 15.9 %collective-permute-start.19 = (bf16[128,512]{1,0:T(8,128)(2,1)S(1)}, bf16[128,512]{1,0:T(8,128)(2,1)S(1)}, u32[]{:S(2)}, u32[]{:S(2)}) collective-permute-start(bf16[128,512]{1,0:T(8,128)(2,1)S(1)} %get-tuple-element.38), channel_id=1, source_target_pairs={{0,8},{2,10},{4,12},{6,14},{8,0},{10,2},{12,4},{14,6},{1,9},{3,11}... | collective-permute-start | bytes 393224 | tf_op jit(solution)/shard_map/ppermute | solution.py:20
  118.9 14.9 %collective-permute-start.20 = (bf16[128,512]{1,0:T(8,128)(2,1)S(1)}, bf16[128,512]{1,0:T(8,128)(2,1)S(1)}, u32[]{:S(2)}, u32[]{:S(2)}) collective-permute-start(bf16[128,512]{1,0:T(8,128)(2,1)S(1)} %get-tuple-element.37), channel_id=1, source_target_pairs={{0,4},{2,6},{4,0},{6,2},{8,12},{10,14},{12,8},{14,10},{1,5},{3,7},... | collective-permute-start | bytes 393224 | tf_op jit(solution)/shard_map/ppermute | solution.py:20
